TPU v7x, 32 devices: a whole 2x2x4 slice. The times are simulated.
32 devices in a mesh: blk: 8 (over z, core), layer: 4 (over y, x).
Axes of the slice: x: 2, y: 2, z: 4, core: 2. Of those that a mesh axis runs over, the one named last changes fastest.
Arguments:
- t2: bfloat16 [1024, 8, 4, 1024], P(None, 'blk', 'layer'), may hold values from -6 to 6
- tile_ids: int32 [8, 4, 8], P('blk', 'layer'), may hold values from 0 to 7, each once within a row
- counts: int32 [8, 4], P('blk', 'layer'), may hold values from 4 to 8, as said below
- integrals: bfloat16 [8, 4, 4, 8, 128, 1024], P('blk', 'layer'), may hold values from -0.09375 to 0.09375
- owner: int32 [8, 4], P('blk'), may hold values from 0 to 3, each once within a row
Outputs:
- residual: bfloat16 [4, 256, 8, 1024], P('layer', None, 'blk')
Inputs may be any that keep to these rules, and one draw needn't show every extreme that they name: Slots j >= counts hold no tile and are ignored; some group is full in every draw.
All inputs are finite; a program needn't handle non-finite values.
Results may differ from a plain program's by a relative error of at most 0.001.
Values may be sent and summed in bfloat16 or wider, within the bound.
A program may use at most 128 MiB of HBM per device.

v0:
```python
import jax
import jax.numpy as jnp
from jax import lax
from jax.sharding import PartitionSpec as P


def shifted(value, axis, steps):
    count = lax.axis_size(axis)
    pairs = [(source, (source + steps) % count) for source in range(count)]
    return lax.ppermute(value, axis, pairs)


def body(t2, tile_ids, counts, integrals, owner):
    row_count = t2.shape[0]
    tile_count = tile_ids.shape[2]
    tile_width = t2.shape[3] // tile_count
    col_count = integrals.shape[5]
    stop_count = integrals.shape[2]
    layer_count = lax.axis_size("layer")
    piece_rows = row_count // layer_count
    slot_index = jnp.arange(tile_count, dtype=jnp.int32)
    select = (tile_ids[0, 0][:, None] == slot_index[None, :]) & (slot_index < counts[0, 0])[:, None]
    packed = t2[:, 0, 0].reshape(row_count, tile_count, tile_width)
    own_panel = jnp.einsum(
        "pjt,jk->pkt", packed, select.astype(jnp.bfloat16), preferred_element_type=jnp.float32
    )
    own_panel = own_panel.astype(jnp.bfloat16).reshape(row_count, tile_count * tile_width)

    def contract(panel_rows, stop_index):
        block = integrals[0, 0, stop_index].reshape(tile_count * tile_width, col_count)
        return jnp.dot(panel_rows, block, preferred_element_type=jnp.float32)

    panels = [own_panel]
    carried = own_panel
    for stop_index in range(1, stop_count):
        carried = shifted(carried, "blk", 1)
        panels.append(carried)
    inverse = jnp.argsort(owner[0])
    summed = contract(panels[0], 0)
    for stop_index in range(1, stop_count):
        summed = summed + contract(panels[stop_index], stop_index)
    partial_value = summed.reshape(layer_count, piece_rows, 1, col_count)
    partial_value = jnp.take(partial_value, inverse, axis=0)
    result = lax.psum_scatter(partial_value, "layer", scatter_dimension=0, tiled=True).astype(
        jnp.bfloat16
    )
    return result


def solution(mesh):
    return jax.shard_map(
        body,
        mesh=mesh,
        in_specs=(
            P(None, "blk", "layer", None),
            P("blk", "layer", None),
            P("blk", "layer"),
            P("blk", "layer", None, None, None, None),
            P("blk", None),
        ),
        out_specs=P("layer", None, "blk", None),
        check_vma=False,
    )
```

profile of v0, /device:TPU:0, one launch (start us, length us, event | category | flops | bytes accessed | tf_op | source)
XLA Modules:
  0.0 169.1 jit_solution(17923470009000077179)
XLA Ops:
  6.5 0.0 reduce-scatter.4.cloned.1.call-start
  6.5 0.0 copy-start
  6.5 2.2 %copy.6 = bf16[128,8,8,128]{3,2,1,0:T(8,128)(2,1)S(1)} copy(bf16[128,8,8,128]{3,1,2,0:T(8,128)(2,1)} %bitcast.39) | data formatting | bytes 4194304
  9.4 0.0 copy-done
  9.4 0.7 convolution_convert_fusion
  10.1 0.0 copy-start.1
  10.2 0.6 copy.10
  10.8 0.5 collective-permute-start
  11.3 27.9 %collective-permute-done = bf16[1024,1024]{1,0:T(8,128)(2,1)} collective-permute-done((bf16[1024,1024]{1,0:T(8,128)(2,1)S(1)}, bf16[1024,1024]{1,0:T(8,128)(2,1)}, u32[]{:S(2)}, u32[]{:S(2)}) %collective-permute-start) | collective-permute-done | bytes 2097184 | tf_op jit(solution)/shard_map/ppermute | solution.py:10
  39.2 0.0 collective-permute-start.1
  39.2 0.0 copy-done.1
  39.2 0.7 sort.17
  39.9 26.8 %collective-permute-done.1 = bf16[1024,1024]{1,0:T(8,128)(2,1)} collective-permute-done((bf16[1024,1024]{1,0:T(8,128)(2,1)}, bf16[1024,1024]{1,0:T(8,128)(2,1)}, u32[]{:S(2)}, u32[]{:S(2)}) %collective-permute-start.1) | collective-permute-done | bytes 2097184 | tf_op jit(solution)/shard_map/ppermute | solution.py:10
  66.7 0.0 collective-permute-start.2
  66.7 3.9 %fusion.6 = (bf16[1,1,1,8,128,1024]{5,4,3,2,1,0:T(8,128)(2,1)S(1)}, bf16[1,1,1,8,128,1024]{5,4,3,2,1,0:T(8,128)(2,1)S(1)}, bf16[1,1,1,8,128,1024]{5,4,3,2,1,0:T(8,128)(2,1)S(1)}, bf16[1,1,1,8,128,1024]{5,4,3,2,1,0:T(8,128)(2,1)S(1)}) fusion(bf16[1,1,4,8,128,1024]{5,4,3,2,1,0:T(8,128)(2,1)} %param.8), kind=kLoop, calls=%fused_computation.15 | loop fusion | bytes 16777216 | tf_op jit(solution)/shard_map/slice | solution.py:30
  70.7 2.3 %fusion.5 = f32[1024,1024]{1,0:T(8,128)S(1)} fusion(bf16[1024,1024]{1,0:T(8,128)(2,1)S(1)} %bitcast.43, bf16[128,8,8,128]{3,2,1,0:T(8,128)(2,1)S(1)} %bitcast.36), kind=kOutput, calls=%fused_computation.14 | convolution fusion | flops 2147483648 | bytes 8388608 | tf_op jit(solution)/shard_map/dot_general | solution.py:31
  73.0 3.9 %fusion.7 = f32[1024,1024]{1,0:T(8,128)S(1)} fusion(bf16[1024,1024]{1,0:T(8,128)(2,1)} %collective-permute-done, bf16[1024,1024]{1,0:T(8,128)(2,1)S(1)} %bitcast.42), kind=kOutput, calls=%fused_computation.16 | convolution fusion | flops 2147483648 | bytes 8388608 | tf_op jit(solution)/shard_map/dot_general | solution.py:31
  76.9 3.9 %fusion.8 = f32[1024,1024]{1,0:T(8,128)S(1)} fusion(bf16[1024,1024]{1,0:T(8,128)(2,1)} %collective-permute-done.1, bf16[1024,1024]{1,0:T(8,128)(2,1)S(1)} %bitcast.41), kind=kOutput, calls=%fused_computation.17 | convolution fusion | flops 2147483648 | bytes 8388608 | tf_op jit(solution)/shard_map/dot_general | solution.py:31
  80.9 13.3 %collective-permute-done.2 = bf16[1024,1024]{1,0:T(8,128)(2,1)S(1)} collective-permute-done((bf16[1024,1024]{1,0:T(8,128)(2,1)}, bf16[1024,1024]{1,0:T(8,128)(2,1)S(1)}, u32[]{:S(2)}, u32[]{:S(2)}) %collective-permute-start.2) | collective-permute-done | bytes 2097184 | tf_op jit(solution)/shard_map/ppermute | solution.py:10
  94.2 4.4 %add_add_fusion = f32[1024,1024]{1,0:T(8,128)} fusion(f32[1024,1024]{1,0:T(8,128)S(1)} %fusion.8, f32[1024,1024]{1,0:T(8,128)S(1)} %fusion.5, f32[1024,1024]{1,0:T(8,128)S(1)} %fusion.7, bf16[1024,1024]{1,0:T(8,128)(2,1)S(1)} %collective-permute-done.2, bf16[1024,1024]{1,0:T(8,128)(2,1)S(1)} %bitcast.38), kind=kOutput, calls=%fused_computation.2 | convolution fusion | flops 2150629376 | bytes 20971520 | tf_op jit(solution)/shard_map/dot_general | solution.py:31
  98.6 5.0 %gather_fusion = f32[4,256,1024]{2,1,0:T(8,128)} fusion(f32[4,256,1024]{2,1,0:T(8,128)} %bitcast.34, s32[1024]{0:T(1024)S(1)} %pad_clamp_fusion), kind=kCustom, calls=%fused_computation | custom fusion | bytes 8388624 | tf_op jit(solution)/shard_map/jit(_take)/gather | solution.py:43
  103.5 5.1 %bitcast_select_fusion = f32[4,256,1,1024]{3,1,2,0:T(8,128)} fusion(f32[4,256,1024]{2,1,0:T(8,128)} %gather_fusion, pred[4]{0:T(512)(128)(4,1)S(1)} %compare_and_fusion), kind=kLoop, calls=%fused_computation.1 | loop fusion | flops 1048576 | bytes 8388612 | tf_op jit(solution)/shard_map/jit(_take)/select_n | solution.py:43
  108.6 0.0 reduce-scatter.4.cloned.1.call-update
  108.6 51.6 %reduce-scatter.4.cloned.1.call-done = f32[1,256,1,1024]{3,1,2,0:T(8,128)} async-done(((f32[4,256,1,1024]{3,1,2,0:T(8,128)}), f32[1,256,1,1024]{3,1,2,0:T(8,128)}) %reduce-scatter.4.cloned.1.call-update) | async-done | bytes 1048592
  160.2 2.1 %convert_element_type.12 = bf16[1,256,1,1024]{3,1,2,0:T(8,128)(2,1)} convert(f32[1,256,1,1024]{3,1,2,0:T(8,128)} %reduce-scatter.4.cloned.1.call-done) | non-fusion elementwise | flops 262144 | bytes 1572864 | tf_op jit(solution)/shard_map/convert_element_type | solution.py:44
  (5 shorter events, 0.0 us)
Async XLA Ops:
  6.5 153.7 %reduce-scatter.4.cloned.1.call-start = ((), (), s32[]{:S(2)}) async-start(), calls=%async_computation.1 | async-start | bytes 5242880
  6.5 2.9 %copy-start = (s32[1,1,8]{2,1,0:T(1,128)S(1)}, s32[1,1,8]{2,1,0:T(1,128)}, u32[]{:S(2)}) copy-start(s32[1,1,8]{2,1,0:T(1,128)} %param.6) | copy-start | bytes 100
  10.1 29.0 %copy-start.1 = (s32[1,4]{1,0:T(1,128)S(1)}, s32[1,4]{1,0:T(1,128)}, u32[]{:S(2)}) copy-start(s32[1,4]{1,0:T(1,128)} %param.9) | copy-start | bytes 52
  10.8 28.4 %collective-permute-start = (bf16[1024,1024]{1,0:T(8,128)(2,1)S(1)}, bf16[1024,1024]{1,0:T(8,128)(2,1)}, u32[]{:S(2)}, u32[]{:S(2)}) collective-permute-start(bf16[1024,1024]{1,0:T(8,128)(2,1)S(1)} %bitcast.40), channel_id=1, source_target_pairs={{0,4},{4,8},{8,12},{12,16},{16,20},{20,24},{24,28},{28,0},{1,5},{5... | collective-permute-start | bytes 6291464 | tf_op jit(solution)/shard_map/ppermute | solution.py:10
  39.2 27.6 %collective-permute-start.1 = (bf16[1024,1024]{1,0:T(8,128)(2,1)}, bf16[1024,1024]{1,0:T(8,128)(2,1)}, u32[]{:S(2)}, u32[]{:S(2)}) collective-permute-start(bf16[1024,1024]{1,0:T(8,128)(2,1)} %collective-permute-done), channel_id=1, source_target_pairs={{0,4},{4,8},{8,12},{12,16},{16,20},{20,24},{24,28},{28,0},{1,5},{5... | collective-permute-start | bytes 6291464 | tf_op jit(solution)/shard_map/ppermute | solution.py:10
  66.7 27.5 %collective-permute-start.2 = (bf16[1024,1024]{1,0:T(8,128)(2,1)}, bf16[1024,1024]{1,0:T(8,128)(2,1)S(1)}, u32[]{:S(2)}, u32[]{:S(2)}) collective-permute-start(bf16[1024,1024]{1,0:T(8,128)(2,1)} %collective-permute-done.1), channel_id=1, source_target_pairs={{0,4},{4,8},{8,12},{12,16},{16,20},{20,24},{24,28},{28,0},{1,5},{5... | collective-permute-start | bytes 6291464 | tf_op jit(solution)/shard_map/ppermute | solution.py:10
Sparse Core Ops, SparseCore 0:
  108.7 51.4 reduce-scatter.3
where the time goes:
time: 169 us
  waiting for transfers between devices  120 us (71%)
  matrix products  15.3 us (9%)
  between operations  14.1 us (8%)
  local copies, waits for them, and re-layouts  11.7 us (7%)
  other arithmetic  7.92 us (5%)
    ppermute x3, waiting for transfers between devices, shifted(): return lax.ppermute(value, axis, pairs)  68 us
    unnamed x2, waiting for transfers between devices  51.6 us
    dot_general x4, matrix products, contract(): return jnp.dot(panel_rows, block, preferred_element_type=jnp.float32)  14.6 us
    select_n x2, other arithmetic, body(): partial_value = jnp.take(partial_value, inverse, axis=0)  5.06 us
    gather x1, local copies, waits for them, and re-layouts, body(): partial_value = jnp.take(partial_value, inverse, axis=0)  4.97 us
    slice x1, local copies, waits for them, and re-layouts, contract(): integrals[0, 0, stop_index].reshape(tile_count * tile_width, col_count)  3.92 us
  transfers between devices with their start and end apart: 4, of which 4 were waited for; matrix products, arithmetic and copies ran while one was open for 9% of the time, Pallas kernels for 0%

commit v1 on v0

v1 whole, which is shorter than its diff:
```python
import functools

import jax
import jax.numpy as jnp
from jax import lax
from jax.experimental import pallas as pl
from jax.experimental.pallas import tpu as pltpu
from jax.sharding import PartitionSpec as P

MESH = pl.DeviceIdType.MESH
LANES = 256
CHUNK_ROWS = 32
ACC_SLOTS = 4


def kernel(
    n_blk,
    n_layer,
    ids_ref,
    counts_ref,
    owner_ref,
    t2_ref,
    ints_ref,
    out_ref,
    packed,
    panels,
    slab,
    acc,
    stage,
    landed,
    t2_sem,
    slab_sem,
    ring_send,
    ring_recv,
    sum_send,
    sum_recv,
):
    stops = ints_ref.shape[0]
    tile_rows, width = t2_ref.shape[1], t2_ref.shape[2]
    cols = ints_ref.shape[2]
    tiles = ids_ref.shape[0]
    tile = width // tiles
    rows = panels.shape[3]
    chunks = tile_rows // rows
    lanes = min(LANES, cols)
    blk, layer = lax.axis_index("blk"), lax.axis_index("layer")
    right, left = lax.rem(blk + 1, n_blk), lax.rem(blk + n_blk - 1, n_blk)
    others = [lax.rem(layer + d, n_layer) for d in range(1, n_layer)]

    t2_copy = pltpu.make_async_copy(t2_ref, packed, t2_sem)
    t2_copy.start()
    slab_copies = [
        pltpu.make_async_copy(ints_ref.at[s], slab.at[s], slab_sem.at[s]) for s in range(stops)
    ]
    for copy in slab_copies:
        copy.start()

    barrier = pltpu.get_barrier_semaphore()
    for neighbour in (left, right):
        pl.semaphore_signal(barrier, inc=1, device_id={"blk": neighbour}, device_id_type=MESH)
    for other in others:
        pl.semaphore_signal(barrier, inc=1, device_id={"layer": other}, device_id_type=MESH)

    count = counts_ref[0]

    def weight(condition, dtype):
        return jnp.full((1, tile), condition.astype(jnp.float32), jnp.float32).astype(dtype)

    def expand(c):
        pieces = [
            packed[:, pl.ds(c * rows, rows), j * tile : (j + 1) * tile].reshape(n_layer * rows, tile)
            for j in range(tiles)
        ]
        for k in range(tiles):
            placed = pieces[0] * held[0][k]
            for j in range(1, tiles):
                placed = placed + pieces[j] * held[j][k]
            panels[0, c, :, :, k * tile : (k + 1) * tile] = placed.reshape(n_layer, rows, tile)

    def to_slots(c):
        for q in range(n_layer):
            for n in range(cols // tile):
                at = slice(n * tile, (n + 1) * tile)
                moved = acc[c % ACC_SLOTS, 0, :, at] * owned[0][q]
                for t in range(1, n_layer):
                    moved = moved + acc[c % ACC_SLOTS, t, :, at] * owned[t][q]
                stage[c, q, :, at] = moved

    def hop(s, c):
        return pltpu.make_async_remote_copy(
            src_ref=panels.at[s, c],
            dst_ref=panels.at[s + 1, c],
            send_sem=ring_send.at[s, c],
            recv_sem=ring_recv.at[s, c],
            device_id={"blk": right},
            device_id_type=MESH,
        )

    def give(d, c):
        return pltpu.make_async_remote_copy(
            src_ref=stage.at[c, others[d]],
            dst_ref=landed.at[d, c],
            send_sem=sum_send.at[d, c],
            recv_sem=sum_recv.at[d, c],
            device_id={"layer": others[d]},
            device_id_type=MESH,
        )

    def multiply(s, c, first):
        @pl.loop(0, cols // lanes)
        def _(n):
            at = pl.ds(pl.multiple_of(n * lanes, lanes), lanes)
            left_side = panels[s, c].reshape(n_layer * rows, width)
            product = jnp.dot(left_side, slab[s, :, at], preferred_element_type=jnp.float32)
            product = product.reshape(n_layer, rows, lanes)
            if first:
                acc[c % ACC_SLOTS, :, :, at] = product
            else:
                acc[c % ACC_SLOTS, :, :, at] += product

    def finish(c):
        for d in range(n_layer - 1):
            give(d, c).wait_recv()
        total = stage[c, layer]
        for d in range(n_layer - 1):
            total = total + landed[d, c]
        out_ref[c * rows : (c + 1) * rows, :] = total.astype(out_ref.dtype)

    held = [
        [weight((ids_ref[j] == k) & (j < count), jnp.bfloat16) for k in range(tiles)]
        for j in range(tiles)
    ]
    owned = [
        [weight(owner_ref[t] == q, jnp.float32) for q in range(n_layer)] for t in range(n_layer)
    ]
    t2_copy.wait()
    for c in range(min(2, chunks)):
        expand(c)
    pl.semaphore_wait(barrier, 2 + n_layer - 1)
    for c in range(min(2, chunks)):
        hop(0, c).start()
    for c in range(2, chunks):
        expand(c)

    hops = stops - 1
    for step in range(chunks + hops - 1):
        for s in range(1, hops):
            c = step - (s - 1)
            if 0 <= c < chunks:
                hop(s - 1, c).wait_recv()
                hop(s, c).start()
        if step + 2 < chunks:
            hop(0, step + 2).start()
        if step == 0:
            slab_copies[0].wait()
        if step < chunks:
            multiply(0, step, True)
        for s in range(1, hops):
            c = step - (s - 1)
            if c == 0:
                slab_copies[s].wait()
            if 0 <= c < chunks:
                multiply(s, c, False)
        c = step - (hops - 1)
        if c == 0:
            slab_copies[hops].wait()
        if 0 <= c < chunks:
            hop(hops - 1, c).wait_recv()
            multiply(hops, c, False)
            to_slots(c)
            for d in range(n_layer - 1):
                give(d, c).start()
        if 0 <= c - 2 < chunks:
            finish(c - 2)
    for c in range(max(chunks - 2, 0), chunks):
        finish(c)
    for c in range(chunks):
        for s in range(hops):
            hop(s, c).wait_send()
        for d in range(n_layer - 1):
            give(d, c).wait_send()


def body(n_blk, n_layer, t2, tile_ids, counts, integrals, owner):
    row_count, width = t2.shape[0], t2.shape[3]
    stops, tiles, tile, cols = integrals.shape[2:]
    tile_rows = row_count // n_layer
    rows = CHUNK_ROWS
    chunks = tile_rows // rows
    hops = stops - 1
    moved = 2 * stops * width * cols + 2 * row_count * width
    result = pl.pallas_call(
        functools.partial(kernel, n_blk, n_layer),
        out_shape=jax.ShapeDtypeStruct((tile_rows, cols), jnp.bfloat16),
        in_specs=[pl.BlockSpec(memory_space=pltpu.SMEM)] * 3 + [pl.BlockSpec(memory_space=pl.ANY)] * 2,
        out_specs=pl.BlockSpec(memory_space=pltpu.VMEM),
        scratch_shapes=[
            pltpu.VMEM((n_layer, tile_rows, width), jnp.bfloat16),
            pltpu.VMEM((stops, chunks, n_layer, rows, width), jnp.bfloat16),
            pltpu.VMEM((stops, width, cols), jnp.bfloat16),
            pltpu.VMEM((ACC_SLOTS, n_layer, rows, cols), jnp.float32),
            pltpu.VMEM((chunks, n_layer, rows, cols), jnp.float32),
            pltpu.VMEM((n_layer - 1, chunks, rows, cols), jnp.float32),
            pltpu.SemaphoreType.DMA,
            pltpu.SemaphoreType.DMA((stops,)),
            pltpu.SemaphoreType.DMA((hops, chunks)),
            pltpu.SemaphoreType.DMA((hops, chunks)),
            pltpu.SemaphoreType.DMA((n_layer - 1, chunks)),
            pltpu.SemaphoreType.DMA((n_layer - 1, chunks)),
        ],
        compiler_params=pltpu.CompilerParams(
            collective_id=0, has_side_effects=True, vmem_limit_bytes=60 * 2**20
        ),
        cost_estimate=pl.CostEstimate(
            flops=2 * stops * row_count * width * cols, bytes_accessed=moved, transcendentals=0
        ),
    )(
        tile_ids.reshape(tiles),
        counts.reshape(1),
        owner.reshape(n_layer),
        t2.reshape(n_layer, tile_rows, width),
        integrals.reshape(stops, tiles * tile, cols),
    )
    return result.reshape(1, tile_rows, 1, cols)


def solution(mesh):
    return jax.shard_map(
        functools.partial(body, mesh.shape["blk"], mesh.shape["layer"]),
        mesh=mesh,
        in_specs=(
            P(None, "blk", "layer", None),
            P("blk", "layer", None),
            P("blk", "layer"),
            P("blk", "layer", None, None, None, None),
            P("blk", None),
        ),
        out_specs=P("layer", None, "blk", None),
        check_vma=False,
    )
```

time: 169 us -> 90.3 us (0.53)
  waiting for transfers between devices: 120 us -> 0 us
  Pallas kernels: 0 us -> 87.6 us
  matrix products: 15.3 us -> 0 us
  between operations: 14.1 us -> 0.66 us
  local copies, waits for them, and re-layouts: 11.7 us -> 1.87 us
  other arithmetic: 7.92 us -> 0 us
    pallas_call x0 -> x1, Pallas kernels: none -> 87.6 us  [body(): pl.pallas_call(functools.partial(kernel, n_blk, n_layer), out_shape=jax.S...]
    ppermute x3 -> x0, waiting for transfers between devices: 68 us -> none  [shifted(): return lax.ppermute(value, axis, pairs)]
    unnamed x2 -> x0, waiting for transfers between devices: 51.6 us -> none
    dot_general x5 -> x0, matrix products: 15.3 us -> none  [the longest x4 14.6 us: contract(): return jnp.dot(panel_rows, block, preferred_element_type=jnp.float32)]
    select_n x2 -> x0, other arithmetic: 5.06 us -> none  [body(): partial_value = jnp.take(partial_value, inverse, axis=0)]
    gather x1 -> x0, local copies, waits for them, and re-layouts: 4.97 us -> none  [body(): partial_value = jnp.take(partial_value, inverse, axis=0)]
    slice x1 -> x0, local copies, waits for them, and re-layouts: 3.92 us -> none  [contract(): integrals[0, 0, stop_index].reshape(tile_count * tile_width, col_count)]
    convert_element_type x1 -> x0, other arithmetic: 2.09 us -> none  [body(): lax.psum_scatter(partial_value, 'layer', scatter_dimension=0, tiled=True)]
  transfers between devices with their start and end apart: 4 -> 0, of which waited for: 4 -> 0; matrix products, arithmetic and copies ran while one was open for 9% -> 0% of each run, Pallas kernels for 0% -> 0%
where the time goes in v1:
time: 90.3 us; the launch traced here: 90.1 us
  Pallas kernels  87.6 us (97%)
  local copies, waits for them, and re-layouts  1.87 us (2%)
    pallas_call x1, Pallas kernels, body(): pl.pallas_call(functools.partial(kernel, n_blk, n_layer), out_shape=jax.S...  87.6 us
    unnamed x1, local copies, waits for them, and re-layouts  1.87 us

profile of v1, /device:TPU:0, one launch (start us, length us, event | category | flops | bytes accessed | tf_op | source)
XLA Modules:
  0.0 90.1 jit_solution(8064086387856646598)
XLA Ops:
  0.7 87.6 %shard_map.55 = bf16[256,1024]{1,0:T(8,128)(2,1)} custom-call(s32[8]{0:T(128)} %bitcast.10, s32[1]{0:T(128)} %bitcast.6.counts_ref, s32[4]{0:T(128)} %bitcast.11, bf16[4,256,1024]{2,1,0:T(8,128)(2,1)} %bitcast.9, bf16[4,1024,1024]{2,1,0:T(8,128)(2,1)} %bitcast.8), custom_call_target="tpu_custom_call" | custom-call | flops 8589934592 | bytes 10485760 | tf_op jit(solution)/shard_map/pallas_call | solution.py:192
  88.2 1.9 %copy.8 = bf16[1,256,1,1024]{3,1,2,0:T(8,128)(2,1)} copy(bf16[1,256,1,1024]{3,1,2,0:T(8,128)(2,1)} %bitcast.7) | data formatting | bytes 1048576

commit v2 on v1

--- a/solution.py
+++ b/solution.py
@@ -9,8 +9,9 @@
 
 MESH = pl.DeviceIdType.MESH
 LANES = 256
-CHUNK_ROWS = 32
 ACC_SLOTS = 4
+AHEAD = 2
+SIXTEENTHS = (1, 2, 2, 2, 2, 2, 2, 1, 1, 1)
 
 
 def kernel(
@@ -22,7 +23,8 @@
     t2_ref,
     ints_ref,
     out_ref,
-    packed,
+    head,
+    rest,
     panels,
     slab,
     acc,
@@ -40,20 +42,13 @@
     cols = ints_ref.shape[2]
     tiles = ids_ref.shape[0]
     tile = width // tiles
-    rows = panels.shape[3]
-    chunks = tile_rows // rows
+    sizes = [part * tile_rows // 16 for part in SIXTEENTHS]
+    starts = [sum(sizes[:c]) for c in range(len(sizes))]
+    chunks = len(sizes)
     lanes = min(LANES, cols)
     blk, layer = lax.axis_index("blk"), lax.axis_index("layer")
     right, left = lax.rem(blk + 1, n_blk), lax.rem(blk + n_blk - 1, n_blk)
     others = [lax.rem(layer + d, n_layer) for d in range(1, n_layer)]
-
-    t2_copy = pltpu.make_async_copy(t2_ref, packed, t2_sem)
-    t2_copy.start()
-    slab_copies = [
-        pltpu.make_async_copy(ints_ref.at[s], slab.at[s], slab_sem.at[s]) for s in range(stops)
-    ]
-    for copy in slab_copies:
-        copy.start()
 
     barrier = pltpu.get_barrier_semaphore()
     for neighbour in (left, right):
@@ -61,35 +56,51 @@
     for other in others:
         pl.semaphore_signal(barrier, inc=1, device_id={"layer": other}, device_id_type=MESH)
 
+    t2_copies = [
+        pltpu.make_async_copy(t2_ref.at[:, pl.ds(0, sizes[0])], head, t2_sem.at[0]),
+        pltpu.make_async_copy(
+            t2_ref.at[:, pl.ds(sizes[0], tile_rows - sizes[0])], rest, t2_sem.at[1]
+        ),
+    ]
+    slab_copies = [
+        pltpu.make_async_copy(ints_ref.at[s], slab.at[s], slab_sem.at[s]) for s in range(stops)
+    ]
+    for copy in t2_copies + slab_copies:
+        copy.start()
+
     count = counts_ref[0]
 
     def weight(condition, dtype):
         return jnp.full((1, tile), condition.astype(jnp.float32), jnp.float32).astype(dtype)
 
+    def span(c):
+        return pl.ds(n_layer * starts[c], n_layer * sizes[c])
+
     def expand(c):
+        source, at = (head, 0) if c == 0 else (rest, starts[c] - sizes[0])
         pieces = [
-            packed[:, pl.ds(c * rows, rows), j * tile : (j + 1) * tile].reshape(n_layer * rows, tile)
+            source[:, pl.ds(at, sizes[c]), j * tile : (j + 1) * tile].reshape(n_layer * sizes[c], tile)
             for j in range(tiles)
         ]
         for k in range(tiles):
             placed = pieces[0] * held[0][k]
             for j in range(1, tiles):
                 placed = placed + pieces[j] * held[j][k]
-            panels[0, c, :, :, k * tile : (k + 1) * tile] = placed.reshape(n_layer, rows, tile)
+            panels[0, span(c), k * tile : (k + 1) * tile] = placed
 
     def to_slots(c):
         for q in range(n_layer):
             for n in range(cols // tile):
                 at = slice(n * tile, (n + 1) * tile)
-                moved = acc[c % ACC_SLOTS, 0, :, at] * owned[0][q]
+                moved = acc[c % ACC_SLOTS, pl.ds(0, sizes[c]), at] * owned[0][q]
                 for t in range(1, n_layer):
-                    moved = moved + acc[c % ACC_SLOTS, t, :, at] * owned[t][q]
-                stage[c, q, :, at] = moved
+                    moved = moved + acc[c % ACC_SLOTS, pl.ds(t * sizes[c], sizes[c]), at] * owned[t][q]
+                stage[q, pl.ds(starts[c], sizes[c]), at] = moved
 
     def hop(s, c):
         return pltpu.make_async_remote_copy(
-            src_ref=panels.at[s, c],
-            dst_ref=panels.at[s + 1, c],
+            src_ref=panels.at[s, span(c)],
+            dst_ref=panels.at[s + 1, span(c)],
             send_sem=ring_send.at[s, c],
             recv_sem=ring_recv.at[s, c],
             device_id={"blk": right},
@@ -98,8 +109,8 @@
 
     def give(d, c):
         return pltpu.make_async_remote_copy(
-            src_ref=stage.at[c, others[d]],
-            dst_ref=landed.at[d, c],
+            src_ref=stage.at[others[d], pl.ds(starts[c], sizes[c])],
+            dst_ref=landed.at[d, pl.ds(starts[c], sizes[c])],
             send_sem=sum_send.at[d, c],
             recv_sem=sum_recv.at[d, c],
             device_id={"layer": others[d]},
@@ -110,21 +121,22 @@
         @pl.loop(0, cols // lanes)
         def _(n):
             at = pl.ds(pl.multiple_of(n * lanes, lanes), lanes)
-            left_side = panels[s, c].reshape(n_layer * rows, width)
-            product = jnp.dot(left_side, slab[s, :, at], preferred_element_type=jnp.float32)
-            product = product.reshape(n_layer, rows, lanes)
+            product = jnp.dot(
+                panels[s, span(c)], slab[s, :, at], preferred_element_type=jnp.float32
+            )
             if first:
-                acc[c % ACC_SLOTS, :, :, at] = product
+                acc[c % ACC_SLOTS, pl.ds(0, n_layer * sizes[c]), at] = product
             else:
-                acc[c % ACC_SLOTS, :, :, at] += product
+                acc[c % ACC_SLOTS, pl.ds(0, n_layer * sizes[c]), at] += product
 
     def finish(c):
         for d in range(n_layer - 1):
             give(d, c).wait_recv()
-        total = stage[c, layer]
+        at = pl.ds(starts[c], sizes[c])
+        total = stage[layer, at]
         for d in range(n_layer - 1):
-            total = total + landed[d, c]
-        out_ref[c * rows : (c + 1) * rows, :] = total.astype(out_ref.dtype)
+            total = total + landed[d, at]
+        out_ref[at, :] = total.astype(out_ref.dtype)
 
     held = [
         [weight((ids_ref[j] == k) & (j < count), jnp.bfloat16) for k in range(tiles)]
@@ -133,14 +145,15 @@
     owned = [
         [weight(owner_ref[t] == q, jnp.float32) for q in range(n_layer)] for t in range(n_layer)
     ]
-    t2_copy.wait()
-    for c in range(min(2, chunks)):
+    t2_copies[0].wait()
+    expand(0)
+    pl.semaphore_wait(barrier, 2 + n_layer - 1)
+    hop(0, 0).start()
+    t2_copies[1].wait()
+    for c in range(1, chunks):
         expand(c)
-    pl.semaphore_wait(barrier, 2 + n_layer - 1)
-    for c in range(min(2, chunks)):
-        hop(0, c).start()
-    for c in range(2, chunks):
-        expand(c)
+        if c < AHEAD:
+            hop(0, c).start()
 
     hops = stops - 1
     for step in range(chunks + hops - 1):
@@ -149,8 +162,8 @@
             if 0 <= c < chunks:
                 hop(s - 1, c).wait_recv()
                 hop(s, c).start()
-        if step + 2 < chunks:
-            hop(0, step + 2).start()
+        if step + AHEAD < chunks:
+            hop(0, step + AHEAD).start()
         if step == 0:
             slab_copies[0].wait()
         if step < chunks:
@@ -185,23 +198,25 @@
     row_count, width = t2.shape[0], t2.shape[3]
     stops, tiles, tile, cols = integrals.shape[2:]
     tile_rows = row_count // n_layer
-    rows = CHUNK_ROWS
-    chunks = tile_rows // rows
+    first = SIXTEENTHS[0] * tile_rows // 16
+    most = max(SIXTEENTHS) * tile_rows // 16
+    chunks = len(SIXTEENTHS)
     hops = stops - 1
     moved = 2 * stops * width * cols + 2 * row_count * width
     result = pl.pallas_call(
         functools.partial(kernel, n_blk, n_layer),
-        out_shape=jax.ShapeDtypeStruct((tile_rows, cols), jnp.bfloat16),
+        out_shape=pltpu.VMEM((tile_rows, cols), jnp.bfloat16),
         in_specs=[pl.BlockSpec(memory_space=pltpu.SMEM)] * 3 + [pl.BlockSpec(memory_space=pl.ANY)] * 2,
         out_specs=pl.BlockSpec(memory_space=pltpu.VMEM),
         scratch_shapes=[
-            pltpu.VMEM((n_layer, tile_rows, width), jnp.bfloat16),
-            pltpu.VMEM((stops, chunks, n_layer, rows, width), jnp.bfloat16),
+            pltpu.VMEM((n_layer, first, width), jnp.bfloat16),
+            pltpu.VMEM((n_layer, tile_rows - first, width), jnp.bfloat16),
+            pltpu.VMEM((stops, row_count, width), jnp.bfloat16),
             pltpu.VMEM((stops, width, cols), jnp.bfloat16),
-            pltpu.VMEM((ACC_SLOTS, n_layer, rows, cols), jnp.float32),
-            pltpu.VMEM((chunks, n_layer, rows, cols), jnp.float32),
-            pltpu.VMEM((n_layer - 1, chunks, rows, cols), jnp.float32),
-            pltpu.SemaphoreType.DMA,
+            pltpu.VMEM((ACC_SLOTS, n_layer * most, cols), jnp.float32),
+            pltpu.VMEM((n_layer, tile_rows, cols), jnp.float32),
+            pltpu.VMEM((n_layer - 1, tile_rows, cols), jnp.float32),
+            pltpu.SemaphoreType.DMA((2,)),
             pltpu.SemaphoreType.DMA((stops,)),
             pltpu.SemaphoreType.DMA((hops, chunks)),
             pltpu.SemaphoreType.DMA((hops, chunks)),

time: 90.3 us -> 86.2 us (0.955)
  Pallas kernels: 87.6 us -> 84.6 us
  local copies, waits for them, and re-layouts: 1.87 us -> 0.8 us
    pallas_call x1, Pallas kernels: 87.6 us -> 84.6 us  [body(): pl.pallas_call(functools.partial(kernel, n_blk, n_layer), out_shape=pltpu...]
    unnamed x1, local copies, waits for them, and re-layouts: 1.87 us -> 0.8 us
where the time goes in v2:
time: 86.2 us; the launch traced here: 86.1 us
  Pallas kernels  84.6 us (98%)
    pallas_call x1, Pallas kernels, body(): pl.pallas_call(functools.partial(kernel, n_blk, n_layer), out_shape=pltpu...  84.6 us

profile of v2, /device:TPU:0, one launch (start us, length us, event | category | flops | bytes accessed | tf_op | source)
XLA Modules:
  0.0 86.1 jit_solution(7026492232608738773)
XLA Ops:
  0.7 84.6 %shard_map.55 = bf16[256,1024]{1,0:T(8,128)(2,1)S(1)} custom-call(s32[8]{0:T(128)} %bitcast.10, s32[1]{0:T(128)} %bitcast.6.counts_ref, s32[4]{0:T(128)} %bitcast.11, bf16[4,256,1024]{2,1,0:T(8,128)(2,1)} %bitcast.9, bf16[4,1024,1024]{2,1,0:T(8,128)(2,1)} %bitcast.8), custom_call_target="tpu_custom_call" | custom-call | flops 8589934592 | bytes 10485760 | tf_op jit(solution)/shard_map/pallas_call | solution.py:206
  85.3 0.8 copy.7

commit v3 on v2

--- a/solution.py
+++ b/solution.py
@@ -157,7 +157,7 @@
 
     hops = stops - 1
     for step in range(chunks + hops - 1):
-        for s in range(1, hops):
+        for s in range(hops - 1, 0, -1):
             c = step - (s - 1)
             if 0 <= c < chunks:
                 hop(s - 1, c).wait_recv()

time: 86.2 us -> 89.2 us (1.035)
  Pallas kernels: 84.6 us -> 87.6 us
    pallas_call x1, Pallas kernels: 84.6 us -> 87.6 us  [body(): pl.pallas_call(functools.partial(kernel, n_blk, n_layer), out_shape=pltpu...]
where the time goes in v3:
time: 89.2 us; the launch traced here: 89.1 us
  Pallas kernels  87.6 us (98%)
    pallas_call x1, Pallas kernels, body(): pl.pallas_call(functools.partial(kernel, n_blk, n_layer), out_shape=pltpu...  87.6 us

profile of v3, /device:TPU:0, one launch (start us, length us, event | category | flops | bytes accessed | tf_op | source)
XLA Modules:
  0.0 89.1 jit_solution(6344403569470542004)
XLA Ops:
  0.7 87.6 %shard_map.55 = bf16[256,1024]{1,0:T(8,128)(2,1)S(1)} custom-call(s32[8]{0:T(128)} %bitcast.10, s32[1]{0:T(128)} %bitcast.6.counts_ref, s32[4]{0:T(128)} %bitcast.11, bf16[4,256,1024]{2,1,0:T(8,128)(2,1)} %bitcast.9, bf16[4,1024,1024]{2,1,0:T(8,128)(2,1)} %bitcast.8), custom_call_target="tpu_custom_call" | custom-call | flops 8589934592 | bytes 10485760 | tf_op jit(solution)/shard_map/pallas_call | solution.py:206
  88.3 0.8 copy.7
